TPU v7x, 256 devices: a whole 4x4x8 slice. The times are simulated.
256 devices in a mesh: tm: 8 (over y, x_lo), space: 32 (over z, x_hi, core).
Axes of the slice: x: 4 (x_hi: 2, x_lo: 2; x = x_hi * 2 + x_lo), y: 4, z: 8, core: 2. Of those that a mesh axis runs over, the one named last changes fastest.
Arguments:
- displace_at_opening: float32 [3, 256, 1024], P(None, 'space'), may hold values from -6 to 6
- resist_at_opening: float32 [256, 1024], P('space'), may hold values from 1 to 2
- operator_main_entries: float32 [256, 1024], P('space'), may hold values from 1 to 3
- thermal_forcing: float32 [3, 256, 1024], P(None, 'space'), may hold values from -6 to 6
- downward_link_matrix: float32 [3, 3, 256, 1024], P(None, None, 'space'), may hold values from 0.1 to 1
- lateral_link_matrix: float32 [3, 3, 256, 1024], P(None, None, 'space'), may hold values from 0.1 to 1
- heat_reading_array: float32 [64], replicated, may hold values from 0.5 to 1.5
- reading_lookup_per_tick: int32 [16], P('tm'), may hold values from 0 to 63
Outputs:
- u_end: float32 [8, 3, 256, 1024], P('tm', None, 'space')
- s_end: float32 [8, 256, 1024], P('tm', 'space')
All inputs are finite; a program needn't handle non-finite values.
Results may differ from a plain program's by a relative error of at most 0.00018.
Values sent between devices are 32-bit elements; how exact they have to be, the bound alone decides.
A program may use at most 64 MiB of HBM per device.

v0:
```python
import functools

import jax
import jax.numpy as jnp
from jax import lax
from jax.experimental import pallas as pl
from jax.experimental.pallas import tpu as pltpu
from jax.sharding import PartitionSpec as P

COUPLING = 0.9 / 6.4
MASS = 0.3
HARDENING = 0.25
SATURATION = 3.0
TICK = 0.5
HALF_WIDTH = 0.9
SWEEPS = 8
ANAND = 4
ROWS = 24
OWN = 8
PLANES = 26
S0, L0, D0, F0, U0 = 0, 9, 18, 19, 22
MESH = pl.DeviceIdType.MESH


def chebyshev_weights():
    weights, w = [], HALF_WIDTH
    for _ in range(SWEEPS - 1):
        nxt = 1.0 / (2.0 / HALF_WIDTH - w)
        weights.append((nxt * w, 2.0 * nxt / HALF_WIDTH))
        w = nxt
    return weights


def at(row):
    if isinstance(row, int):
        return pl.ds(8 * row, 8)
    return pl.ds(pl.multiple_of(8 * row, 8), 8)


def span(row, count):
    if isinstance(row, int):
        return pl.ds(8 * row, 8 * count)
    return pl.ds(pl.multiple_of(8 * row, 8), 8 * count)


def kernel(
    n_tm, n_sp,
    u_in, s_in, d_in, f_in, down_in, lat_in, heat, look,
    u_out, s_out,
    raw, U, Pd, Z, E, GU, C, VOUT, VIN, CIN, XH, TH, ssem, rsem,
):
    n = lax.axis_index("tm")
    sp = lax.axis_index("space")
    up, dn = lax.rem(sp + n_sp - 1, n_sp), lax.rem(sp + 1, n_sp)
    lane = lax.broadcasted_iota(jnp.int32, (8, 128), 1)
    sub = lax.broadcasted_iota(jnp.int32, (8, 128), 0)
    first_lane, last_lane = lane == 0, lane == 127

    barrier = pltpu.get_barrier_semaphore()
    peers = [(lax.rem(n + d, n_tm), sp) for d in range(1, n_tm)]
    for d in (0, 1, 2, n_tm - 2, n_tm - 1):
        for side in (up, dn):
            peers.append((lax.rem(n + d, n_tm), side))
    for peer in peers:
        pl.semaphore_signal(barrier, inc=1, device_id=peer, device_id_type=MESH)

    def copy(src, dst, sem, who):
        return pltpu.make_async_remote_copy(
            src_ref=src, dst_ref=dst, send_sem=ssem.at[sem], recv_sem=rsem.at[sem],
            device_id=who, device_id_type=MESH,
        )

    def pack(plane, tile_of):
        for c in range(8):
            raw[plane, pl.ds(8 * OWN + c, 8, stride=8), :] = tile_of(pl.ds(128 * c, 128))

    for a in range(3):
        for b in range(3):
            pack(S0 + 3 * a + b, lambda cols, a=a, b=b: down_in[a, b, :, cols])
            pack(L0 + 3 * a + b, lambda cols, a=a, b=b: lat_in[a, b, :, cols])
        pack(F0 + a, lambda cols, a=a: f_in[a, :, cols])
        pack(U0 + a, lambda cols, a=a: u_in[a, :, cols])
    pack(D0, lambda cols: d_in[:, cols])
    pack(U0 + 3, lambda cols: s_in[:, cols])
    for k in range(2):
        TH[n, pl.ds(8 * k, 8), :] = jnp.full((8, 128), heat[look[k]], jnp.float32)

    pl.semaphore_wait(barrier, len(peers))

    own_raw = raw.at[:, span(OWN, 8), :]
    halos = [
        copy(own_raw, raw.at[:, span(0, 8), :], 0, (n, dn)),
        copy(own_raw, raw.at[:, span(16, 8), :], 1, (n, up)),
    ]
    heats = [
        copy(TH.at[n], TH.at[n], 1 + d, (lax.rem(n + d, n_tm), sp)) for d in range(1, n_tm)
    ]
    for c in halos + heats:
        c.start()
    for d in range(1, n_tm):
        src = lax.rem(n + n_tm - d, n_tm)
        copy(TH.at[src], TH.at[src], 1 + d, (src, sp)).wait_recv()
    for c in halos:
        c.wait()
    for c in heats:
        c.wait_send()

    def east(v):
        a = pltpu.roll(v, 127, 1)
        return jnp.where(last_lane, pltpu.roll(a, 7, 0), a)

    def west(v):
        a = pltpu.roll(v, 1, 1)
        return jnp.where(first_lane, pltpu.roll(a, 1, 0), a)

    corner = (lane == 127) & (sub == 7)

    def build(r, diag):
        below = raw[D0, at(jnp.minimum(r + 1, ROWS - 1)), :]
        seam = ((sp == 0) & (r == OWN - 1)) | ((sp == n_sp - 1) & (r == 2 * OWN - 1))
        cs = COUPLING * jnp.minimum(diag, below) * jnp.where(seam, 0.0, 1.0)
        cl = jnp.where(corner, 0.0, COUPLING * jnp.minimum(diag, east(diag)))
        for k in range(9):
            raw[S0 + k, at(r), :] = raw[S0 + k, at(r), :] * cs
            raw[L0 + k, at(r), :] = raw[L0 + k, at(r), :] * cl
        for k in range(4):
            U[k, at(r), :] = raw[U0 + k, at(r), :]
        raw[D0, at(r), :] = 1.0 / diag
        return below

    lax.fori_loop(0, ROWS, build, raw[D0, at(0), :])

    def heat_of(slice_index, tick):
        return TH[slice_index, pl.ds(8 * tick, 1), :]

    def mean_heat(slice_index):
        return 0.5 * (TH[slice_index, 0:1, :] + TH[slice_index, 8:9, :])

    def creep(load, store_s, t, h, lo, count, chunk):
        rate = jnp.exp(2.0 - 2.0 / t)

        def body(i, _):
            r = lo + i * chunk
            u0, u1, u2, s = (load(k, r, chunk) for k in range(4))
            q2 = (u0 * u0 + u1 * u1 + u2 * u2) * (1.0 / 3.0) + 1.0
            qi = lax.rsqrt(q2)
            q = q2 * qi
            x = s
            for _ in range(ANAND):
                x = s + (h * HARDENING) * rate * jnp.tanh(q / x) * (1.0 - x * (1.0 / SATURATION))
            E[span(r, chunk), :] = (h * rate) * jnp.tanh(q / x) * qi
            store_s(r, chunk, x)
            return 0

        lax.fori_loop(0, count // chunk, body, 0)

    def stencil(load, lo, hi, emit):
        p = [load(b, lo - 1) for b in range(3)]
        s = [[raw[S0 + 3 * a + b, at(lo - 1), :] for b in range(3)] for a in range(3)]
        north = [s[0][b] * p[0] + s[1][b] * p[1] + s[2][b] * p[2] for b in range(3)]
        p = [load(b, lo) for b in range(3)]
        for r in range(lo, hi):
            nxt = [load(b, r + 1) for b in range(3)]
            s = [[raw[S0 + 3 * a + b, at(r), :] for b in range(3)] for a in range(3)]
            l = [[raw[L0 + 3 * a + b, at(r), :] for b in range(3)] for a in range(3)]
            pe = [east(p[b]) for b in range(3)]
            wf = [west(l[0][b] * p[0] + l[1][b] * p[1] + l[2][b] * p[2]) for b in range(3)]
            cv = []
            for a in range(3):
                south = s[a][0] * nxt[0] + s[a][1] * nxt[1] + s[a][2] * nxt[2]
                right = l[a][0] * pe[0] + l[a][1] * pe[1] + l[a][2] * pe[2]
                cv.append((north[a] + wf[a]) + (south + right))
            north = [s[0][b] * p[0] + s[1][b] * p[1] + s[2][b] * p[2] for b in range(3)]
            emit(r, p, cv)
            p = nxt

    def force(r, v, cv, th):
        inv, e = raw[D0, at(r), :], E[at(r), :]
        return [
            inv * (th * raw[F0 + a, at(r), :] - e * v[a] - cv[a]) for a in range(3)
        ]

    def fine_tick(t):
        h = TICK

        def load(k, r, c):
            return U[k, span(r, c), :]

        def store_s(r, c, x):
            U[3, span(r, c), :] = x

        creep(load, store_s, t, h, 0, ROWS, 8)
        th = h * t

        def first(r, v, cv):
            g = force(r, v, cv, th)
            for a in range(3):
                z = g[a] - (1.0 - MASS) * v[a]
                Z[a, at(r), :] = z
                Pd[a, at(r), :] = z
                if OWN <= r < 2 * OWN:
                    U[a, at(r), :] = v[a] + z

        stencil(lambda b, r: U[b, at(r), :], 1, ROWS - 1, first)
        for k, (alpha, beta) in enumerate(chebyshev_weights()):
            def sweep(r, v, cv, alpha=alpha, beta=beta, k=k):
                inv = raw[D0, at(r), :]
                for a in range(3):
                    z = Z[a, at(r), :] - v[a] - inv * cv[a]
                    p = alpha * v[a] + beta * z
                    if k < SWEEPS - 2:
                        Z[a, at(r), :] = z
                        Pd[a, at(r), :] = p
                    if OWN <= r < 2 * OWN:
                        U[a, at(r), :] = U[a, at(r), :] + p

            stencil(lambda b, r: Pd[b, at(r), :], 2 + k, ROWS - 2 - k, sweep)

    def exchange(slot, sem, planes):
        own = U.at[pl.ds(0, planes), span(OWN, 8), :]
        pair = [
            copy(own, XH.at[slot, 0, pl.ds(0, planes)], sem, (n, dn)),
            copy(own, XH.at[slot, 1, pl.ds(0, planes)], sem + 1, (n, up)),
        ]
        for c in pair:
            c.start()
        for c in pair:
            c.wait()
        for k in range(planes):
            U[k, span(0, 8), :] = XH[slot, 0, k]
            U[k, span(16, 8), :] = XH[slot, 1, k]

    def coarse_own():
        t = mean_heat(n)

        def load(k, r, c):
            return U[k, span(r, c), :]

        def store_s(r, c, x):
            GU[3, span(r - OWN, c), :] = x

        creep(load, store_s, t, 2.0 * TICK, OWN, 8, 8)

        def emit(r, v, cv):
            g = force(r, v, cv, 2.0 * TICK * t)
            for a in range(3):
                GU[a, at(r - OWN), :] = MASS * v[a] + g[a]

        stencil(lambda b, r: U[b, at(r), :], OWN, 2 * OWN, emit)

    def coarse_step(m, _):
        t = mean_heat(m)

        def load(k, r, c):
            return U[k, span(r, c), :]

        def store_s(r, c, x):
            U[3, span(r, c), :] = x

        creep(load, store_s, t, 2.0 * TICK, 0, ROWS, 8)

        def emit(r, v, cv):
            g = force(r, v, cv, 2.0 * TICK * t)
            for a in range(3):
                U[a, at(r), :] = MASS * v[a] + g[a]

        stencil(lambda b, r: U[b, at(r), :], 1, ROWS - 1, emit)
        return 0

    lax.fori_loop(0, n, coarse_step, 0)

    @pl.when(n > 0)
    def _():
        coarse_own()
        exchange(0, 9, 4)

    odd = lax.rem(n, 2) == 1
    even = (lax.rem(n, 2) == 0) & (n > 0)

    def to_next(p):
        nxt = lax.rem(n + 1, n_tm)
        base = 17 + 6 * p
        return [
            copy(VOUT.at[p], VIN.at[p, :, span(OWN, 8), :], base, (nxt, sp)),
            copy(VOUT.at[p], VIN.at[p, :, span(16, 8), :], base + 1, (nxt, up)),
            copy(VOUT.at[p], VIN.at[p, :, span(0, 8), :], base + 2, (nxt, dn)),
        ]

    def to_second(p):
        nxt = lax.rem(n + 2, n_tm)
        base = 20 + 6 * p
        return [
            copy(VOUT.at[p], VIN.at[p, :, span(OWN, 8), :], base, (nxt, sp)),
            copy(VOUT.at[p, :, span(0, 2), :], VIN.at[p, :, span(16, 2), :], base + 1, (nxt, up)),
            copy(VOUT.at[p, :, span(6, 2), :], VIN.at[p, :, span(6, 2), :], base + 2, (nxt, dn)),
        ]

    def corrections(p):
        nxt = lax.rem(n + 1, n_tm)
        base = 29 + 3 * p
        return [
            copy(C.at[p], CIN.at[p, :, span(OWN, 8), :], base, (nxt, sp)),
            copy(C.at[p, :, span(0, 1), :], CIN.at[p, :, span(16, 1), :], base + 1, (nxt, up)),
            copy(C.at[p, :, span(7, 1), :], CIN.at[p, :, span(7, 1), :], base + 2, (nxt, dn)),
        ]

    def one_pass(p, _):
        @pl.when((n > 0) | (p == 0))
        def _():
            def tick(i, _):
                @pl.when(i == 1)
                def _():
                    exchange(1 + 2 * p, 11 + 4 * p, 3)

                fine_tick(heat_of(n, i))
                return 0

            lax.fori_loop(0, 2, tick, 0)

        @pl.when(n > 0)
        def _():
            for a in range(3):
                C[p, a] = U[a, span(OWN, 8), :] - GU[a]
            C[p, 3] = U[3, span(OWN, 8), :] / GU[3]

        @pl.when(odd & (n < n_tm - 1))
        def _():
            for c in corrections(p):
                c.start()

        @pl.when(odd)
        def _():
            for c in to_next(p):
                c.wait_recv()
            for k in range(4):
                for r in range(3):
                    U[k, span(8 * r, 8), :] = VIN[p, k, span(8 * r, 8), :]

        @pl.when(even)
        def _():
            for c in to_second(p):
                c.wait_recv()
            for c in corrections(p):
                c.wait_recv()
            t = mean_heat(n - 1)

            def load(k, r, c):
                return VIN[p, k, span(r, c), :]

            def store_s(r, c, x):
                U[3, span(r, c), :] = x * CIN[p, 3, span(r, c), :]

            creep(load, store_s, t, 2.0 * TICK, OWN - 1, 10, 10)

            def emit(r, v, cv):
                g = force(r, v, cv, 2.0 * TICK * t)
                for a in range(3):
                    U[a, at(r), :] = MASS * v[a] + g[a] + CIN[p, a, at(r), :]

            stencil(lambda b, r: VIN[p, b, at(r), :], OWN - 1, 2 * OWN + 1, emit)

        @pl.when(n == 0)
        def _():
            for k in range(4):
                VOUT[p, k] = U[k, span(OWN, 8), :]

        @pl.when(n > 0)
        def _():
            coarse_own()
            for a in range(3):
                VOUT[p, a] = GU[a] + C[p, a]
            VOUT[p, 3] = GU[3] * C[p, 3]

        @pl.when(jnp.logical_not(odd))
        def _():
            for c in to_next(p):
                c.start()

        @pl.when(jnp.logical_not(odd) & (n < n_tm - 2))
        def _():
            for c in to_second(p):
                c.start()

        @pl.when(even & (p == 0))
        def _():
            exchange(2, 13, 4)

        return 0

    lax.fori_loop(0, 2, one_pass, 0)

    for c in range(8):
        cols = pl.ds(128 * c, 128)
        for a in range(3):
            u_out[0, a, :, cols] = VOUT[1, a, pl.ds(c, 8, stride=8), :]
        s_out[0, :, cols] = VOUT[1, 3, pl.ds(c, 8, stride=8), :]

    for p in range(2):
        @pl.when(odd & (n < n_tm - 1))
        def _():
            for c in corrections(p):
                c.wait_send()

        @pl.when(jnp.logical_not(odd))
        def _():
            for c in to_next(p):
                c.wait_send()

        @pl.when(jnp.logical_not(odd) & (n < n_tm - 2))
        def _():
            for c in to_second(p):
                c.wait_send()


def per_device(n_tm, n_sp, u, s, d, f, down, lat, heat, look):
    vmem = pl.BlockSpec(memory_space=pltpu.VMEM)
    smem = pl.BlockSpec(memory_space=pltpu.SMEM)
    f32 = jnp.float32
    return pl.pallas_call(
        functools.partial(kernel, n_tm, n_sp),
        out_shape=(
            jax.ShapeDtypeStruct((1, 3, 8, 1024), f32),
            jax.ShapeDtypeStruct((1, 8, 1024), f32),
        ),
        in_specs=[vmem] * 6 + [smem] * 2,
        out_specs=(vmem, vmem),
        scratch_shapes=[
            pltpu.VMEM((PLANES, 8 * ROWS, 128), f32),
            pltpu.VMEM((4, 8 * ROWS, 128), f32),
            pltpu.VMEM((3, 8 * ROWS, 128), f32),
            pltpu.VMEM((3, 8 * ROWS, 128), f32),
            pltpu.VMEM((8 * ROWS, 128), f32),
            pltpu.VMEM((4, 64, 128), f32),
            pltpu.VMEM((2, 4, 64, 128), f32),
            pltpu.VMEM((2, 4, 64, 128), f32),
            pltpu.VMEM((2, 4, 8 * ROWS, 128), f32),
            pltpu.VMEM((2, 4, 8 * ROWS, 128), f32),
            pltpu.VMEM((4, 2, 4, 64, 128), f32),
            pltpu.VMEM((8, 16, 128), f32),
            pltpu.SemaphoreType.DMA((35,)),
            pltpu.SemaphoreType.DMA((35,)),
        ],
        compiler_params=pltpu.CompilerParams(
            collective_id=0, has_side_effects=True, vmem_limit_bytes=32 * 1024 * 1024
        ),
        name="parareal",
    )(u, s, d, f, down, lat, heat, look)


def solution(mesh):
    return jax.shard_map(
        functools.partial(per_device, mesh.shape["tm"], mesh.shape["space"]),
        mesh=mesh,
        in_specs=(
            P(None, "space", None),
            P("space", None),
            P("space", None),
            P(None, "space", None),
            P(None, None, "space", None),
            P(None, None, "space", None),
            P(),
            P("tm"),
        ),
        out_specs=(P("tm", None, "space", None), P("tm", "space", None)),
        check_vma=False,
    )
```

profile of v0, /device:TPU:26, one launch (start us, length us, event | category | flops | bytes accessed | tf_op | source)
XLA Modules:
  0.0 104.7 jit_solution(1868853992107523230)
XLA Ops:
  0.6 0.0 copy-start
  0.6 1.0 copy-done
  1.6 0.0 copy-start.1
  1.6 1.0 copy-done.1
  2.6 0.0 copy-start.2
  2.6 0.9 copy-done.2
  3.5 0.0 copy-start.3
  3.5 0.9 copy-done.3
  4.3 0.0 copy-start.4
  4.3 0.8 copy-done.4
  5.1 0.0 copy-start.5
  5.1 0.8 copy-done.5
  5.9 0.0 copy-start.6
  5.9 0.7 copy-done.6
  6.5 0.0 copy-start.7
  6.5 0.7 copy-done.7
  7.2 96.2 %parareal.1 = (f32[1,3,8,1024]{3,2,1,0:T(8,128)S(1)}, f32[1,8,1024]{2,1,0:T(8,128)S(1)}) custom-call(f32[3,8,1024]{2,1,0:T(8,128)S(1)} %copy-done.2, f32[8,1024]{1,0:T(8,128)S(1)} %copy-done.4, f32[8,1024]{1,0:T(8,128)S(1)} %copy-done.5, f32[3,8,1024]{2,1,0:T(8,128)S(1)} %copy-done.3, f32[3,3,8,1024]{3,2,1,0:T(8,128)S(1)} %copy-done, ...), custom_call_target="tpu_custom_call" | custom-call | tf_op jit(solution)/shard_map/parareal/pallas_call | solution.py:419
  103.4 0.6 copy.12
  104.1 0.6 copy.13
Async XLA Ops:
  0.6 1.0 copy-start
  1.6 1.0 copy-start.1
  2.6 0.9 copy-start.2
  3.5 0.9 copy-start.3
  4.3 0.8 copy-start.4
  5.1 0.8 copy-start.5
  5.9 0.7 copy-start.6
  6.5 0.7 copy-start.7
where the time goes:
time: 105 us
  Pallas kernels  96.2 us (92%)
  local copies, waits for them, and re-layouts  7.78 us (7%)
    pallas_call x1, Pallas kernels, per_device(): pl.pallas_call(functools.partial(kernel, n_tm, n_sp), out_shape=(jax.Shap...  96.2 us
    unnamed x18, local copies, waits for them, and re-layouts  7.78 us

commit v1 on v0

--- a/solution.py
+++ b/solution.py
@@ -15,10 +15,11 @@
 HALF_WIDTH = 0.9
 SWEEPS = 8
 ANAND = 4
-ROWS = 24
-OWN = 8
+ROWS = 26
+OWN = 9
+ABOVE, BELOW = 1, 17
 PLANES = 26
-S0, L0, D0, F0, U0 = 0, 9, 18, 19, 22
+S0, D0, U0, F0, L0 = 0, 9, 10, 14, 17
 MESH = pl.DeviceIdType.MESH
 
 
@@ -45,22 +46,35 @@
 
 def kernel(
     n_tm, n_sp,
+    u_hbm, s_hbm, d_hbm, f_hbm, down_hbm, lat_hbm, heat_hbm, look_hbm,
+    u_out, s_out,
     u_in, s_in, d_in, f_in, down_in, lat_in, heat, look,
-    u_out, s_out,
-    raw, U, Pd, Z, E, GU, C, VOUT, VIN, CIN, XH, TH, ssem, rsem,
+    raw, DI, U, Pd, Z, E, GU, C, VOUT, VIN, CIN, XH, TH, lsem, ssem, rsem,
 ):
     n = lax.axis_index("tm")
     sp = lax.axis_index("space")
     up, dn = lax.rem(sp + n_sp - 1, n_sp), lax.rem(sp + 1, n_sp)
+    up2, dn2 = lax.rem(sp + n_sp - 2, n_sp), lax.rem(sp + 2, n_sp)
     lane = lax.broadcasted_iota(jnp.int32, (8, 128), 1)
     sub = lax.broadcasted_iota(jnp.int32, (8, 128), 0)
     first_lane, last_lane = lane == 0, lane == 127
+
+    loads = [
+        pltpu.make_async_copy(src, dst, lsem.at[k])
+        for k, (src, dst) in enumerate(
+            [(look_hbm, look), (heat_hbm, heat), (down_hbm, down_in), (lat_hbm, lat_in),
+             (u_hbm, u_in), (s_hbm, s_in), (d_hbm, d_in), (f_hbm, f_in)]
+        )
+    ]
+    for c in loads:
+        c.start()
 
     barrier = pltpu.get_barrier_semaphore()
     peers = [(lax.rem(n + d, n_tm), sp) for d in range(1, n_tm)]
     for d in (0, 1, 2, n_tm - 2, n_tm - 1):
         for side in (up, dn):
             peers.append((lax.rem(n + d, n_tm), side))
+    peers += [(n, up2), (n, dn2)]
     for peer in peers:
         pl.semaphore_signal(barrier, inc=1, device_id=peer, device_id_type=MESH)
 
@@ -74,6 +88,8 @@
         for c in range(8):
             raw[plane, pl.ds(8 * OWN + c, 8, stride=8), :] = tile_of(pl.ds(128 * c, 128))
 
+    for c in loads:
+        c.wait()
     for a in range(3):
         for b in range(3):
             pack(S0 + 3 * a + b, lambda cols, a=a, b=b: down_in[a, b, :, cols])
@@ -87,22 +103,51 @@
 
     pl.semaphore_wait(barrier, len(peers))
 
-    own_raw = raw.at[:, span(OWN, 8), :]
-    halos = [
-        copy(own_raw, raw.at[:, span(0, 8), :], 0, (n, dn)),
-        copy(own_raw, raw.at[:, span(16, 8), :], 1, (n, up)),
+    core = lax.rem(sp, 2)
+    y = n // 2
+    sibling = sp + 1 - 2 * core
+    outer = jnp.where(core == 0, up, dn)
+    to_sibling = jnp.where(core == 0, ABOVE, BELOW)
+    to_outer = jnp.where(core == 0, BELOW, ABOVE)
+    from_outer = jnp.where(core == 0, ABOVE, BELOW)
+    across = (n + 1 - 2 * lax.rem(n, 2), outer)
+    shared = copy(raw.at[:, span(OWN + y, 1), :], raw.at[:, span(to_outer + y, 1), :], 1, across)
+    shared.start()
+    straight = [
+        copy(raw.at[:, span(OWN + 4, 4), :], raw.at[:, span(to_outer + 4, 4), :], 2, across),
+        copy(raw.at[:, span(OWN, 8), :], raw.at[:, span(to_sibling, 8), :], 0, (n, sibling)),
+        copy(
+            raw.at[pl.ds(0, F0 - 1), span(OWN + 7, 1), :],
+            raw.at[pl.ds(0, F0 - 1), span(0, 1), :], 6, (n, dn2),
+        ),
+        copy(
+            raw.at[pl.ds(D0, 4), span(OWN, 1), :],
+            raw.at[pl.ds(D0, 4), span(ROWS - 1, 1), :], 7, (n, up2),
+        ),
     ]
     heats = [
-        copy(TH.at[n], TH.at[n], 1 + d, (lax.rem(n + d, n_tm), sp)) for d in range(1, n_tm)
+        copy(TH.at[n], TH.at[n], 7 + d, (lax.rem(n + d, n_tm), sp)) for d in range(1, n_tm)
     ]
-    for c in halos + heats:
+    for c in straight + heats:
+        c.start()
+    shared.wait_recv()
+    passed = raw.at[:, span(from_outer + y, 1), :]
+    passing = [
+        copy(passed, passed, 2 + d, (lax.rem(n + 2 * d, n_tm), sp)) for d in (1, 2, 3)
+    ]
+    for c in passing:
         c.start()
     for d in range(1, n_tm):
         src = lax.rem(n + n_tm - d, n_tm)
-        copy(TH.at[src], TH.at[src], 1 + d, (src, sp)).wait_recv()
-    for c in halos:
+        copy(TH.at[src], TH.at[src], 7 + d, (src, sp)).wait_recv()
+    for c in straight:
         c.wait()
-    for c in heats:
+    for d in (1, 2, 3):
+        src = lax.rem(n + n_tm - 2 * d, n_tm)
+        row = raw.at[:, span(from_outer + src // 2, 1), :]
+        copy(row, row, 2 + d, (src, sp)).wait_recv()
+    shared.wait_send()
+    for c in heats + passing:
         c.wait_send()
 
     def east(v):
@@ -114,21 +159,23 @@
         return jnp.where(first_lane, pltpu.roll(a, 1, 0), a)
 
     corner = (lane == 127) & (sub == 7)
-
-    def build(r, diag):
-        below = raw[D0, at(jnp.minimum(r + 1, ROWS - 1)), :]
-        seam = ((sp == 0) & (r == OWN - 1)) | ((sp == n_sp - 1) & (r == 2 * OWN - 1))
-        cs = COUPLING * jnp.minimum(diag, below) * jnp.where(seam, 0.0, 1.0)
-        cl = jnp.where(corner, 0.0, COUPLING * jnp.minimum(diag, east(diag)))
-        for k in range(9):
-            raw[S0 + k, at(r), :] = raw[S0 + k, at(r), :] * cs
-            raw[L0 + k, at(r), :] = raw[L0 + k, at(r), :] * cl
-        for k in range(4):
+    for r in range(ROWS):
+        diag = raw[D0, at(r), :]
+        if r < ROWS - 1:
+            row = 8 * sp + (r - OWN)
+            seam = (row == -1) | (row == 8 * n_sp - 1)
+            below = raw[D0, at(r + 1), :]
+            cs = COUPLING * jnp.minimum(diag, below) * jnp.where(seam, 0.0, 1.0)
+            for k in range(9):
+                raw[S0 + k, at(r), :] = raw[S0 + k, at(r), :] * cs
+        if 0 < r < ROWS - 1:
+            cl = jnp.where(corner, 0.0, COUPLING * jnp.minimum(diag, east(diag)))
+            for k in range(9):
+                raw[L0 + k, at(r), :] = raw[L0 + k, at(r), :] * cl
+            DI[at(r), :] = 1.0 / diag
+            U[3, at(r), :] = raw[U0 + 3, at(r), :]
+        for k in range(3):
             U[k, at(r), :] = raw[U0 + k, at(r), :]
-        raw[D0, at(r), :] = 1.0 / diag
-        return below
-
-    lax.fori_loop(0, ROWS, build, raw[D0, at(0), :])
 
     def heat_of(slice_index, tick):
         return TH[slice_index, pl.ds(8 * tick, 1), :]
@@ -175,7 +222,7 @@
             p = nxt
 
     def force(r, v, cv, th):
-        inv, e = raw[D0, at(r), :], E[at(r), :]
+        inv, e = DI[at(r), :], E[at(r), :]
         return [
             inv * (th * raw[F0 + a, at(r), :] - e * v[a] - cv[a]) for a in range(3)
         ]
@@ -189,7 +236,7 @@
         def store_s(r, c, x):
             U[3, span(r, c), :] = x
 
-        creep(load, store_s, t, h, 0, ROWS, 8)
+        creep(load, store_s, t, h, 1, ROWS - 2, 8)
         th = h * t
 
         def first(r, v, cv):
@@ -198,25 +245,25 @@
                 z = g[a] - (1.0 - MASS) * v[a]
                 Z[a, at(r), :] = z
                 Pd[a, at(r), :] = z
-                if OWN <= r < 2 * OWN:
+                if OWN <= r < OWN + 8:
                     U[a, at(r), :] = v[a] + z
 
-        stencil(lambda b, r: U[b, at(r), :], 1, ROWS - 1, first)
+        stencil(lambda b, r: U[b, at(r), :], 2, ROWS - 2, first)
         for k, (alpha, beta) in enumerate(chebyshev_weights()):
             def sweep(r, v, cv, alpha=alpha, beta=beta, k=k):
-                inv = raw[D0, at(r), :]
+                inv = DI[at(r), :]
                 for a in range(3):
                     z = Z[a, at(r), :] - v[a] - inv * cv[a]
                     p = alpha * v[a] + beta * z
                     if k < SWEEPS - 2:
                         Z[a, at(r), :] = z
                         Pd[a, at(r), :] = p
-                    if OWN <= r < 2 * OWN:
+                    if OWN <= r < OWN + 8:
                         U[a, at(r), :] = U[a, at(r), :] + p
 
-            stencil(lambda b, r: Pd[b, at(r), :], 2 + k, ROWS - 2 - k, sweep)
-
-    def exchange(slot, sem, planes):
+            stencil(lambda b, r: Pd[b, at(r), :], 3 + k, ROWS - 3 - k, sweep)
+
+    def exchange(slot, sem, planes, between=None):
         own = U.at[pl.ds(0, planes), span(OWN, 8), :]
         pair = [
             copy(own, XH.at[slot, 0, pl.ds(0, planes)], sem, (n, dn)),
@@ -224,11 +271,13 @@
         ]
         for c in pair:
             c.start()
+        if between is not None:
+            between()
         for c in pair:
             c.wait()
         for k in range(planes):
-            U[k, span(0, 8), :] = XH[slot, 0, k]
-            U[k, span(16, 8), :] = XH[slot, 1, k]
+            U[k, span(ABOVE, 8), :] = XH[slot, 0, k]
+            U[k, span(BELOW, 8), :] = XH[slot, 1, k]
 
     def coarse_own():
         t = mean_heat(n)
@@ -246,7 +295,7 @@
             for a in range(3):
                 GU[a, at(r - OWN), :] = MASS * v[a] + g[a]
 
-        stencil(lambda b, r: U[b, at(r), :], OWN, 2 * OWN, emit)
+        stencil(lambda b, r: U[b, at(r), :], OWN, OWN + 8, emit)
 
     def coarse_step(m, _):
         t = mean_heat(m)
@@ -257,7 +306,7 @@
         def store_s(r, c, x):
             U[3, span(r, c), :] = x
 
-        creep(load, store_s, t, 2.0 * TICK, 0, ROWS, 8)
+        creep(load, store_s, t, 2.0 * TICK, 1, ROWS - 2, 8)
 
         def emit(r, v, cv):
             g = force(r, v, cv, 2.0 * TICK * t)
@@ -269,39 +318,45 @@
 
     lax.fori_loop(0, n, coarse_step, 0)
 
-    @pl.when(n > 0)
+    @pl.when(n == 1)
     def _():
         coarse_own()
-        exchange(0, 9, 4)
+
+    @pl.when(n > 1)
+    def _():
+        exchange(0, 15, 4, coarse_own)
 
     odd = lax.rem(n, 2) == 1
     even = (lax.rem(n, 2) == 0) & (n > 0)
 
-    def to_next(p):
+    def to_next(p, rows):
         nxt = lax.rem(n + 1, n_tm)
-        base = 17 + 6 * p
+        base = 23 + 6 * p
+        top, low = span(0, rows), span(8 - rows, rows)
         return [
             copy(VOUT.at[p], VIN.at[p, :, span(OWN, 8), :], base, (nxt, sp)),
-            copy(VOUT.at[p], VIN.at[p, :, span(16, 8), :], base + 1, (nxt, up)),
-            copy(VOUT.at[p], VIN.at[p, :, span(0, 8), :], base + 2, (nxt, dn)),
+            copy(VOUT.at[p, :, top, :], VIN.at[p, :, span(BELOW, rows), :], base + 1, (nxt, up)),
+            copy(VOUT.at[p, :, low, :], VIN.at[p, :, span(OWN - rows, rows), :], base + 2, (nxt, dn)),
         ]
 
     def to_second(p):
         nxt = lax.rem(n + 2, n_tm)
-        base = 20 + 6 * p
+        base = 26 + 6 * p
+        top, low = span(0, 2), span(6, 2)
         return [
+            copy(VOUT.at[p, :, top, :], VIN.at[p, :, span(BELOW, 2), :], base + 1, (nxt, up)),
+            copy(VOUT.at[p, :, low, :], VIN.at[p, :, span(OWN - 2, 2), :], base + 2, (nxt, dn)),
             copy(VOUT.at[p], VIN.at[p, :, span(OWN, 8), :], base, (nxt, sp)),
-            copy(VOUT.at[p, :, span(0, 2), :], VIN.at[p, :, span(16, 2), :], base + 1, (nxt, up)),
-            copy(VOUT.at[p, :, span(6, 2), :], VIN.at[p, :, span(6, 2), :], base + 2, (nxt, dn)),
         ]
 
     def corrections(p):
         nxt = lax.rem(n + 1, n_tm)
-        base = 29 + 3 * p
+        base = 35 + 3 * p
+        top, low = span(0, 1), span(7, 1)
         return [
+            copy(C.at[p, :, top, :], CIN.at[p, :, span(BELOW, 1), :], base + 1, (nxt, up)),
+            copy(C.at[p, :, low, :], CIN.at[p, :, span(OWN - 1, 1), :], base + 2, (nxt, dn)),
             copy(C.at[p], CIN.at[p, :, span(OWN, 8), :], base, (nxt, sp)),
-            copy(C.at[p, :, span(0, 1), :], CIN.at[p, :, span(16, 1), :], base + 1, (nxt, up)),
-            copy(C.at[p, :, span(7, 1), :], CIN.at[p, :, span(7, 1), :], base + 2, (nxt, dn)),
         ]
 
     def one_pass(p, _):
@@ -310,7 +365,7 @@
             def tick(i, _):
                 @pl.when(i == 1)
                 def _():
-                    exchange(1 + 2 * p, 11 + 4 * p, 3)
+                    exchange(1 + 2 * p, 17 + 4 * p, 3)
 
                 fine_tick(heat_of(n, i))
                 return 0
@@ -328,13 +383,21 @@
             for c in corrections(p):
                 c.start()
 
-        @pl.when(odd)
-        def _():
-            for c in to_next(p):
+        @pl.when(odd & (p == 0))
+        def _():
+            for c in to_next(p, 8):
                 c.wait_recv()
             for k in range(4):
-                for r in range(3):
-                    U[k, span(8 * r, 8), :] = VIN[p, k, span(8 * r, 8), :]
+                for r in (ABOVE, OWN, BELOW):
+                    U[k, span(r, 8), :] = VIN[p, k, span(r, 8), :]
+
+        @pl.when(odd & (p == 1))
+        def _():
+            for c in to_next(p, 1):
+                c.wait_recv()
+            for k in range(4):
+                for r in range(OWN - 1, OWN + 9):
+                    U[k, at(r), :] = VIN[p, k, at(r), :]
 
         @pl.when(even)
         def _():
@@ -357,7 +420,7 @@
                 for a in range(3):
                     U[a, at(r), :] = MASS * v[a] + g[a] + CIN[p, a, at(r), :]
 
-            stencil(lambda b, r: VIN[p, b, at(r), :], OWN - 1, 2 * OWN + 1, emit)
+            stencil(lambda b, r: VIN[p, b, at(r), :], OWN - 1, OWN + 9, emit)
 
         @pl.when(n == 0)
         def _():
@@ -371,19 +434,20 @@
                 VOUT[p, a] = GU[a] + C[p, a]
             VOUT[p, 3] = GU[3] * C[p, 3]
 
-        @pl.when(jnp.logical_not(odd))
-        def _():
-            for c in to_next(p):
-                c.start()
-
         @pl.when(jnp.logical_not(odd) & (n < n_tm - 2))
         def _():
             for c in to_second(p):
                 c.start()
 
+        for q, rows in ((0, 8), (1, 1)):
+            @pl.when(jnp.logical_not(odd) & (p == q))
+            def _():
+                for c in to_next(q, rows):
+                    c.start()
+
         @pl.when(even & (p == 0))
         def _():
-            exchange(2, 13, 4)
+            exchange(2, 19, 4)
 
         return 0
 
@@ -403,7 +467,7 @@
 
         @pl.when(jnp.logical_not(odd))
         def _():
-            for c in to_next(p):
+            for c in to_next(p, (8, 1)[p]):
                 c.wait_send()
 
         @pl.when(jnp.logical_not(odd) & (n < n_tm - 2))
@@ -414,18 +478,22 @@
 
 def per_device(n_tm, n_sp, u, s, d, f, down, lat, heat, look):
     vmem = pl.BlockSpec(memory_space=pltpu.VMEM)
-    smem = pl.BlockSpec(memory_space=pltpu.SMEM)
+    hbm = pl.BlockSpec(memory_space=pl.ANY)
     f32 = jnp.float32
+    inputs = (u, s, d, f, down, lat)
     return pl.pallas_call(
         functools.partial(kernel, n_tm, n_sp),
         out_shape=(
             jax.ShapeDtypeStruct((1, 3, 8, 1024), f32),
             jax.ShapeDtypeStruct((1, 8, 1024), f32),
         ),
-        in_specs=[vmem] * 6 + [smem] * 2,
+        in_specs=[hbm] * 8,
         out_specs=(vmem, vmem),
-        scratch_shapes=[
+        scratch_shapes=[pltpu.VMEM(x.shape, f32) for x in inputs] + [
+            pltpu.SMEM(heat.shape, f32),
+            pltpu.SMEM(look.shape, jnp.int32),
             pltpu.VMEM((PLANES, 8 * ROWS, 128), f32),
+            pltpu.VMEM((8 * ROWS, 128), f32),
             pltpu.VMEM((4, 8 * ROWS, 128), f32),
             pltpu.VMEM((3, 8 * ROWS, 128), f32),
             pltpu.VMEM((3, 8 * ROWS, 128), f32),
@@ -437,11 +505,12 @@
             pltpu.VMEM((2, 4, 8 * ROWS, 128), f32),
             pltpu.VMEM((4, 2, 4, 64, 128), f32),
             pltpu.VMEM((8, 16, 128), f32),
-            pltpu.SemaphoreType.DMA((35,)),
-            pltpu.SemaphoreType.DMA((35,)),
+            pltpu.SemaphoreType.DMA((8,)),
+            pltpu.SemaphoreType.DMA((41,)),
+            pltpu.SemaphoreType.DMA((41,)),
         ],
         compiler_params=pltpu.CompilerParams(
-            collective_id=0, has_side_effects=True, vmem_limit_bytes=32 * 1024 * 1024
+            collective_id=0, has_side_effects=True, vmem_limit_bytes=60 * 1024 * 1024
         ),
         name="parareal",
     )(u, s, d, f, down, lat, heat, look)

time: 105 us -> 82.6 us (0.79)
  Pallas kernels: 96.2 us -> 79.6 us
  local copies, waits for them, and re-layouts: 7.78 us -> 2.16 us
    pallas_call x1, Pallas kernels: 96.2 us -> 79.6 us  [per_device(): pl.pallas_call(functools.partial(kernel, n_tm, n_sp), out_shape=(jax.Shap...]
    unnamed x18 -> x4, local copies, waits for them, and re-layouts: 7.78 us -> 2.16 us
where the time goes in v1:
time: 82.6 us; the launch traced here: 82.5 us
  Pallas kernels  79.6 us (96%)
  local copies, waits for them, and re-layouts  2.16 us (3%)
    pallas_call x1, Pallas kernels, per_device(): pl.pallas_call(functools.partial(kernel, n_tm, n_sp), out_shape=(jax.Shap...  79.6 us
    unnamed x4, local copies, waits for them, and re-layouts  2.16 us

profile of v1, /device:TPU:26, one launch (start us, length us, event | category | flops | bytes accessed | tf_op | source)
XLA Modules:
  0.0 82.5 jit_solution(4290481132036950284)
XLA Ops:
  0.6 79.6 %parareal.1 = (f32[1,3,8,1024]{3,2,1,0:T(8,128)}, f32[1,8,1024]{2,1,0:T(8,128)}) custom-call(f32[3,8,1024]{2,1,0:T(8,128)} %u_hbm.1, f32[8,1024]{1,0:T(8,128)} %s_hbm.1, f32[8,1024]{1,0:T(8,128)} %d_hbm.1, f32[3,8,1024]{2,1,0:T(8,128)} %f_hbm.1, f32[3,3,8,1024]{3,2,1,0:T(8,128)} %down_hbm.1, f32[3,3,8,1024]{3,2,1,0:T(8,128)} %lat_hbm.1, f32[64]{0:T(128)} %heat_hbm.1, ...), custom_call_target="tpu_custom_call" | custom-call | tf_op jit(solution)/shard_map/parareal/pallas_call | solution.py:484
  80.3 0.0 copy-start
  80.3 1.5 %copy.12 = f32[1,3,8,1024]{3,2,1,0:T(8,128)} copy(f32[1,3,8,1024]{3,2,1,0:T(8,128)} %get-tuple-element.4) | data formatting | bytes 196608
  81.8 0.0 copy-done
  81.8 0.6 copy.13
Async XLA Ops:
  80.3 1.6 %copy-start = (f32[1,8,1024]{2,1,0:T(8,128)S(1)}, f32[1,8,1024]{2,1,0:T(8,128)}, u32[]{:S(2)}) copy-start(f32[1,8,1024]{2,1,0:T(8,128)} %get-tuple-element.5) | copy-start | bytes 98308

commit v2 on v1

--- a/solution.py
+++ b/solution.py
@@ -49,7 +49,7 @@
     u_hbm, s_hbm, d_hbm, f_hbm, down_hbm, lat_hbm, heat_hbm, look_hbm,
     u_out, s_out,
     u_in, s_in, d_in, f_in, down_in, lat_in, heat, look,
-    raw, DI, U, Pd, Z, E, GU, C, VOUT, VIN, CIN, XH, TH, lsem, ssem, rsem,
+    raw, DI, U, W, Pd, Z, E, GU, C, VOUT, VIN, CIN, XH, TH, lsem, ssem, rsem,
 ):
     n = lax.axis_index("tm")
     sp = lax.axis_index("space")
@@ -71,7 +71,7 @@
 
     barrier = pltpu.get_barrier_semaphore()
     peers = [(lax.rem(n + d, n_tm), sp) for d in range(1, n_tm)]
-    for d in (0, 1, 2, n_tm - 2, n_tm - 1):
+    for d in (0, 1, 2, 3, n_tm - 3, n_tm - 2, n_tm - 1):
         for side in (up, dn):
             peers.append((lax.rem(n + d, n_tm), side))
     peers += [(n, up2), (n, dn2)]
@@ -327,7 +327,8 @@
         exchange(0, 15, 4, coarse_own)
 
     odd = lax.rem(n, 2) == 1
-    even = (lax.rem(n, 2) == 0) & (n > 0)
+    sender = lax.rem(n, 2) == 0
+    even = sender & (n > 0)
 
     def to_next(p, rows):
         nxt = lax.rem(n + 1, n_tm)
@@ -359,6 +360,39 @@
             copy(C.at[p], CIN.at[p, :, span(OWN, 8), :], base, (nxt, sp)),
         ]
 
+    last = n_tm - 1
+
+    def trimmed(src, dst, rows, base, who):
+        return [
+            copy(src.at[:, span(0, rows), :], dst.at[:, span(BELOW, rows), :], base + 1, (who, up)),
+            copy(
+                src.at[:, span(8 - rows, rows), :], dst.at[:, span(OWN - rows, rows), :],
+                base + 2, (who, dn),
+            ),
+            copy(src, dst.at[:, span(OWN, 8), :], base, (who, sp)),
+        ]
+
+    def end_to_last():
+        return trimmed(VOUT.at[1], VIN.at[1], 3, 41, last)
+
+    def correction_to_last(back):
+        if back == 2:
+            return trimmed(C.at[1], CIN.at[1], 2, 44, last)
+        return trimmed(C.at[1], CIN.at[0], 1, 47, last)
+
+    def corrected(load, corr, dst, t, lo, count):
+        def store_s(r, c, x):
+            dst[3, span(r, c), :] = x * corr[3, span(r, c), :]
+
+        creep(load, store_s, t, 2.0 * TICK, lo, count, count)
+
+        def emit(r, v, cv):
+            g = force(r, v, cv, 2.0 * TICK * t)
+            for a in range(3):
+                dst[a, at(r), :] = MASS * v[a] + g[a] + corr[a, at(r), :]
+
+        stencil(lambda b, r: load(b, r, 1), lo, lo + count, emit)
+
     def one_pass(p, _):
         @pl.when((n > 0) | (p == 0))
         def _():
@@ -391,63 +425,90 @@
                 for r in (ABOVE, OWN, BELOW):
                     U[k, span(r, 8), :] = VIN[p, k, span(r, 8), :]
 
-        @pl.when(odd & (p == 1))
-        def _():
-            for c in to_next(p, 1):
+        for back in (2, 1):
+            @pl.when((n == last - back) & (p == 1))
+            def _():
+                for c in correction_to_last(back):
+                    c.start()
+
+        @pl.when((n == last) & (p == 1))
+        def _():
+            for c in end_to_last() + correction_to_last(2) + correction_to_last(1):
                 c.wait_recv()
+            corrected(
+                lambda k, r, c: VIN[1, k, span(r, c), :], CIN.at[1], W,
+                mean_heat(last - 2), OWN - 2, 12,
+            )
+            corrected(
+                lambda k, r, c: W[k, span(r, c), :], CIN.at[0], U,
+                mean_heat(last - 1), OWN - 1, 10,
+            )
+
+        @pl.when(odd & (n < last) & (p == 1))
+        def _():
+            @pl.when(n > 1)
+            def _():
+                for c in to_next(p, 1):
+                    c.wait_recv()
+
+            q = jnp.where(n == 1, 0, p)
             for k in range(4):
                 for r in range(OWN - 1, OWN + 9):
-                    U[k, at(r), :] = VIN[p, k, at(r), :]
+                    U[k, at(r), :] = VIN[q, k, at(r), :]
 
         @pl.when(even)
         def _():
-            for c in to_second(p):
-                c.wait_recv()
+            @pl.when((n > 2) | (p == 0))
+            def _():
+                for c in to_second(p):
+                    c.wait_recv()
+
             for c in corrections(p):
                 c.wait_recv()
-            t = mean_heat(n - 1)
-
-            def load(k, r, c):
-                return VIN[p, k, span(r, c), :]
-
-            def store_s(r, c, x):
-                U[3, span(r, c), :] = x * CIN[p, 3, span(r, c), :]
-
-            creep(load, store_s, t, 2.0 * TICK, OWN - 1, 10, 10)
-
-            def emit(r, v, cv):
-                g = force(r, v, cv, 2.0 * TICK * t)
-                for a in range(3):
-                    U[a, at(r), :] = MASS * v[a] + g[a] + CIN[p, a, at(r), :]
-
-            stencil(lambda b, r: VIN[p, b, at(r), :], OWN - 1, OWN + 9, emit)
+            q = jnp.where(n == 2, 0, p)
+            corrected(
+                lambda k, r, c: VIN[q, k, span(r, c), :], CIN.at[p], U,
+                mean_heat(n - 1), OWN - 1, 10,
+            )
 
         @pl.when(n == 0)
         def _():
             for k in range(4):
                 VOUT[p, k] = U[k, span(OWN, 8), :]
 
-        @pl.when(n > 0)
-        def _():
-            coarse_own()
-            for a in range(3):
-                VOUT[p, a] = GU[a] + C[p, a]
-            VOUT[p, 3] = GU[3] * C[p, 3]
-
-        @pl.when(jnp.logical_not(odd) & (n < n_tm - 2))
-        def _():
-            for c in to_second(p):
-                c.start()
-
-        for q, rows in ((0, 8), (1, 1)):
-            @pl.when(jnp.logical_not(odd) & (p == q))
+        def pass_on():
+            @pl.when(n > 0)
             def _():
-                for c in to_next(q, rows):
+                coarse_own()
+                for a in range(3):
+                    VOUT[p, a] = GU[a] + C[p, a]
+                VOUT[p, 3] = GU[3] * C[p, 3]
+
+            @pl.when(sender & (n < n_tm - 2) & ((n > 0) | (p == 0)))
+            def _():
+                for c in to_second(p):
                     c.start()
 
-        @pl.when(even & (p == 0))
-        def _():
-            exchange(2, 19, 4)
+            @pl.when((n == last - 3) & (p == 1))
+            def _():
+                for c in end_to_last():
+                    c.start()
+
+            for q, rows in ((0, 8), (1, 1)):
+                @pl.when(sender & (p == q) & (((n > 0) & (n < last - 1)) | (p == 0)))
+                def _():
+                    for c in to_next(q, rows):
+                        c.start()
+
+        halo_now = even & (p == 0)
+
+        @pl.when(halo_now)
+        def _():
+            exchange(2, 19, 4, pass_on)
+
+        @pl.when(jnp.logical_not(halo_now))
+        def _():
+            pass_on()
 
         return 0
 
@@ -465,14 +526,25 @@
             for c in corrections(p):
                 c.wait_send()
 
-        @pl.when(jnp.logical_not(odd))
+        @pl.when(sender & (((n > 0) & (n < last - 1)) | (p == 0)))
         def _():
             for c in to_next(p, (8, 1)[p]):
                 c.wait_send()
 
-        @pl.when(jnp.logical_not(odd) & (n < n_tm - 2))
+        @pl.when(sender & (n < n_tm - 2) & ((n > 0) | (p == 0)))
         def _():
             for c in to_second(p):
+                c.wait_send()
+
+    @pl.when(n == last - 3)
+    def _():
+        for c in end_to_last():
+            c.wait_send()
+
+    for back in (2, 1):
+        @pl.when(n == last - back)
+        def _():
+            for c in correction_to_last(back):
                 c.wait_send()
 
 
@@ -495,6 +567,7 @@
             pltpu.VMEM((PLANES, 8 * ROWS, 128), f32),
             pltpu.VMEM((8 * ROWS, 128), f32),
             pltpu.VMEM((4, 8 * ROWS, 128), f32),
+            pltpu.VMEM((4, 8 * ROWS, 128), f32),
             pltpu.VMEM((3, 8 * ROWS, 128), f32),
             pltpu.VMEM((3, 8 * ROWS, 128), f32),
             pltpu.VMEM((8 * ROWS, 128), f32),
@@ -506,8 +579,8 @@
             pltpu.VMEM((4, 2, 4, 64, 128), f32),
             pltpu.VMEM((8, 16, 128), f32),
             pltpu.SemaphoreType.DMA((8,)),
-            pltpu.SemaphoreType.DMA((41,)),
-            pltpu.SemaphoreType.DMA((41,)),
+            pltpu.SemaphoreType.DMA((50,)),
+            pltpu.SemaphoreType.DMA((50,)),
         ],
         compiler_params=pltpu.CompilerParams(
             collective_id=0, has_side_effects=True, vmem_limit_bytes=60 * 1024 * 1024

time: 82.6 us -> 78 us (0.944)
  Pallas kernels: 79.6 us -> 75.1 us
    pallas_call x1, Pallas kernels: 79.6 us -> 75.1 us  [per_device(): pl.pallas_call(functools.partial(kernel, n_tm, n_sp), out_shape=(jax.Shap...]
where the time goes in v2:
time: 78 us; the launch traced here: 77.9 us
  Pallas kernels  75.1 us (96%)
  local copies, waits for them, and re-layouts  2.16 us (3%)
    pallas_call x1, Pallas kernels, per_device(): pl.pallas_call(functools.partial(kernel, n_tm, n_sp), out_shape=(jax.Shap...  75.1 us
    unnamed x4, local copies, waits for them, and re-layouts  2.16 us

profile of v2, /device:TPU:26, one launch (start us, length us, event | category | flops | bytes accessed | tf_op | source)
XLA Modules:
  0.0 77.9 jit_solution(11767758125949727464)
XLA Ops:
  0.6 75.1 %parareal.1 = (f32[1,3,8,1024]{3,2,1,0:T(8,128)}, f32[1,8,1024]{2,1,0:T(8,128)}) custom-call(f32[3,8,1024]{2,1,0:T(8,128)} %u_hbm.1, f32[8,1024]{1,0:T(8,128)} %s_hbm.1, f32[8,1024]{1,0:T(8,128)} %d_hbm.1, f32[3,8,1024]{2,1,0:T(8,128)} %f_hbm.1, f32[3,3,8,1024]{3,2,1,0:T(8,128)} %down_hbm.1, f32[3,3,8,1024]{3,2,1,0:T(8,128)} %lat_hbm.1, f32[64]{0:T(128)} %heat_hbm.1, ...), custom_call_target="tpu_custom_call" | custom-call | tf_op jit(solution)/shard_map/parareal/pallas_call | solution.py:556
  75.7 0.0 copy-start
  75.7 1.5 %copy.12 = f32[1,3,8,1024]{3,2,1,0:T(8,128)} copy(f32[1,3,8,1024]{3,2,1,0:T(8,128)} %get-tuple-element.4) | data formatting | bytes 196608
  77.2 0.0 copy-done
  77.2 0.6 copy.13
Async XLA Ops:
  75.7 1.6 %copy-start = (f32[1,8,1024]{2,1,0:T(8,128)S(1)}, f32[1,8,1024]{2,1,0:T(8,128)}, u32[]{:S(2)}) copy-start(f32[1,8,1024]{2,1,0:T(8,128)} %get-tuple-element.5) | copy-start | bytes 98308

commit v3 on v1

--- a/solution.py
+++ b/solution.py
@@ -328,36 +328,54 @@
 
     odd = lax.rem(n, 2) == 1
     even = (lax.rem(n, 2) == 0) & (n > 0)
-
-    def to_next(p, rows):
+    hands_on = odd & (n < n_tm - 1)
+    joins = odd & (n > 1)
+
+    def trimmed(src, dst, rows, base, who):
+        return [
+            copy(src.at[:, span(0, rows), :], dst.at[:, span(BELOW, rows), :], base + 1, (who, up)),
+            copy(
+                src.at[:, span(8 - rows, rows), :], dst.at[:, span(OWN - rows, rows), :],
+                base + 2, (who, dn),
+            ),
+            copy(src, dst.at[:, span(OWN, 8), :], base, (who, sp)),
+        ]
+
+    def whole_halo(base, who):
+        return copy(VOUT.at[0], VIN.at[0, :, span(to_outer, 8), :], base, (who, outer))
+
+    def beside(slot):
+        own = VIN.at[slot, :, span(OWN, 8), :]
+        return copy(own, VIN.at[0, :, span(to_sibling, 8), :], 25, (n, sibling))
+
+    def to_first():
+        return trimmed(VOUT.at[0], VIN.at[1], 1, 41, 1) + [whole_halo(44, 1)]
+
+    def to_next(p):
         nxt = lax.rem(n + 1, n_tm)
-        base = 23 + 6 * p
-        top, low = span(0, rows), span(8 - rows, rows)
-        return [
-            copy(VOUT.at[p], VIN.at[p, :, span(OWN, 8), :], base, (nxt, sp)),
-            copy(VOUT.at[p, :, top, :], VIN.at[p, :, span(BELOW, rows), :], base + 1, (nxt, up)),
-            copy(VOUT.at[p, :, low, :], VIN.at[p, :, span(OWN - rows, rows), :], base + 2, (nxt, dn)),
-        ]
+        if p == 0:
+            own = copy(VOUT.at[0], VIN.at[0, :, span(OWN, 8), :], 23, (nxt, sp))
+            return [own, whole_halo(24, nxt)]
+        return trimmed(VOUT.at[1], VIN.at[1], 1, 29, nxt)
 
     def to_second(p):
-        nxt = lax.rem(n + 2, n_tm)
-        base = 26 + 6 * p
-        top, low = span(0, 2), span(6, 2)
-        return [
-            copy(VOUT.at[p, :, top, :], VIN.at[p, :, span(BELOW, 2), :], base + 1, (nxt, up)),
-            copy(VOUT.at[p, :, low, :], VIN.at[p, :, span(OWN - 2, 2), :], base + 2, (nxt, dn)),
-            copy(VOUT.at[p], VIN.at[p, :, span(OWN, 8), :], base, (nxt, sp)),
-        ]
+        return trimmed(VOUT.at[p], VIN.at[p], 2, 26 + 6 * p, lax.rem(n + 2, n_tm))
 
     def corrections(p):
-        nxt = lax.rem(n + 1, n_tm)
-        base = 35 + 3 * p
-        top, low = span(0, 1), span(7, 1)
-        return [
-            copy(C.at[p, :, top, :], CIN.at[p, :, span(BELOW, 1), :], base + 1, (nxt, up)),
-            copy(C.at[p, :, low, :], CIN.at[p, :, span(OWN - 1, 1), :], base + 2, (nxt, dn)),
-            copy(C.at[p], CIN.at[p, :, span(OWN, 8), :], base, (nxt, sp)),
-        ]
+        return trimmed(C.at[p], CIN.at[p], 1, 35 + 3 * p, lax.rem(n + 1, n_tm))
+
+    def corrected(load, corr, dst, t, lo, count):
+        def store_s(r, c, x):
+            dst[3, span(r, c), :] = x * corr[3, span(r, c), :]
+
+        creep(load, store_s, t, 2.0 * TICK, lo, count, count)
+
+        def emit(r, v, cv):
+            g = force(r, v, cv, 2.0 * TICK * t)
+            for a in range(3):
+                dst[a, at(r), :] = MASS * v[a] + g[a] + corr[a, at(r), :]
+
+        stencil(lambda b, r: load(b, r, 1), lo, lo + count, emit)
 
     def one_pass(p, _):
         @pl.when((n > 0) | (p == 0))
@@ -378,76 +396,97 @@
                 C[p, a] = U[a, span(OWN, 8), :] - GU[a]
             C[p, 3] = U[3, span(OWN, 8), :] / GU[3]
 
-        @pl.when(odd & (n < n_tm - 1))
+        @pl.when(even)
         def _():
             for c in corrections(p):
                 c.start()
 
-        @pl.when(odd & (p == 0))
-        def _():
-            for c in to_next(p, 8):
+        @pl.when((n == 1) & (p == 0))
+        def _():
+            for c in to_first()[:3]:
                 c.wait_recv()
+
+        @pl.when(even & (p == 0))
+        def _():
+            own, halo = to_next(0)
+            own.wait_recv()
+            pair = beside(0)
+            pair.start()
+            pair.wait()
+            halo.wait_recv()
             for k in range(4):
                 for r in (ABOVE, OWN, BELOW):
-                    U[k, span(r, 8), :] = VIN[p, k, span(r, 8), :]
-
-        @pl.when(odd & (p == 1))
-        def _():
-            for c in to_next(p, 1):
+                    U[k, span(r, 8), :] = VIN[0, k, span(r, 8), :]
+
+        @pl.when(even & (p == 1))
+        def _():
+            for c in to_next(1):
                 c.wait_recv()
+
+        @pl.when((n == 1) | (even & (p == 1)))
+        def _():
             for k in range(4):
-                for r in range(OWN - 1, OWN + 9):
-                    U[k, at(r), :] = VIN[p, k, at(r), :]
-
-        @pl.when(even)
-        def _():
+                U[k, span(OWN - 1, 10), :] = VIN[1, k, span(OWN - 1, 10), :]
+
+        @pl.when(joins)
+        def _():
+            for c in corrections(p):
+                c.wait_recv()
             for c in to_second(p):
                 c.wait_recv()
-            for c in corrections(p):
-                c.wait_recv()
-            t = mean_heat(n - 1)
-
-            def load(k, r, c):
-                return VIN[p, k, span(r, c), :]
-
-            def store_s(r, c, x):
-                U[3, span(r, c), :] = x * CIN[p, 3, span(r, c), :]
-
-            creep(load, store_s, t, 2.0 * TICK, OWN - 1, 10, 10)
-
-            def emit(r, v, cv):
-                g = force(r, v, cv, 2.0 * TICK * t)
-                for a in range(3):
-                    U[a, at(r), :] = MASS * v[a] + g[a] + CIN[p, a, at(r), :]
-
-            stencil(lambda b, r: VIN[p, b, at(r), :], OWN - 1, OWN + 9, emit)
+            corrected(
+                lambda k, r, c: VIN[p, k, span(r, c), :], CIN.at[p], U,
+                mean_heat(n - 1), OWN - 1, 10,
+            )
 
         @pl.when(n == 0)
         def _():
             for k in range(4):
                 VOUT[p, k] = U[k, span(OWN, 8), :]
 
-        @pl.when(n > 0)
-        def _():
-            coarse_own()
-            for a in range(3):
-                VOUT[p, a] = GU[a] + C[p, a]
-            VOUT[p, 3] = GU[3] * C[p, 3]
-
-        @pl.when(jnp.logical_not(odd) & (n < n_tm - 2))
-        def _():
-            for c in to_second(p):
-                c.start()
-
-        for q, rows in ((0, 8), (1, 1)):
-            @pl.when(jnp.logical_not(odd) & (p == q))
+        def pass_on():
+            @pl.when(n > 0)
             def _():
-                for c in to_next(q, rows):
+                coarse_own()
+                for a in range(3):
+                    VOUT[p, a] = GU[a] + C[p, a]
+                VOUT[p, 3] = GU[3] * C[p, 3]
+
+            @pl.when((n == 0) & (p == 0))
+            def _():
+                for c in to_first():
                     c.start()
 
-        @pl.when(even & (p == 0))
-        def _():
-            exchange(2, 19, 4)
+            @pl.when(hands_on)
+            def _():
+                for c in to_second(p):
+                    c.start()
+
+            for q in range(2):
+                @pl.when(hands_on & (p == q))
+                def _():
+                    for c in to_next(q):
+                        c.start()
+
+        halo_now = joins & (p == 0)
+
+        @pl.when(halo_now)
+        def _():
+            exchange(2, 19, 4, pass_on)
+
+        @pl.when(jnp.logical_not(halo_now))
+        def _():
+            pass_on()
+
+        @pl.when((n == 1) & (p == 0))
+        def _():
+            pair = beside(1)
+            pair.start()
+            pair.wait()
+            to_first()[3].wait_recv()
+            for k in range(4):
+                for r in (ABOVE, BELOW):
+                    U[k, span(r, 8), :] = VIN[0, k, span(r, 8), :]
 
         return 0
 
@@ -459,20 +498,20 @@
             u_out[0, a, :, cols] = VOUT[1, a, pl.ds(c, 8, stride=8), :]
         s_out[0, :, cols] = VOUT[1, 3, pl.ds(c, 8, stride=8), :]
 
+    @pl.when(n == 0)
+    def _():
+        for c in to_first():
+            c.wait_send()
+
     for p in range(2):
-        @pl.when(odd & (n < n_tm - 1))
+        @pl.when(even)
         def _():
             for c in corrections(p):
                 c.wait_send()
 
-        @pl.when(jnp.logical_not(odd))
-        def _():
-            for c in to_next(p, (8, 1)[p]):
-                c.wait_send()
-
-        @pl.when(jnp.logical_not(odd) & (n < n_tm - 2))
-        def _():
-            for c in to_second(p):
+        @pl.when(hands_on)
+        def _():
+            for c in to_next(p) + to_second(p):
                 c.wait_send()
 
 
@@ -506,8 +545,8 @@
             pltpu.VMEM((4, 2, 4, 64, 128), f32),
             pltpu.VMEM((8, 16, 128), f32),
             pltpu.SemaphoreType.DMA((8,)),
-            pltpu.SemaphoreType.DMA((41,)),
-            pltpu.SemaphoreType.DMA((41,)),
+            pltpu.SemaphoreType.DMA((45,)),
+            pltpu.SemaphoreType.DMA((45,)),
         ],
         compiler_params=pltpu.CompilerParams(
             collective_id=0, has_side_effects=True, vmem_limit_bytes=60 * 1024 * 1024

time: 82.6 us -> 75.4 us (0.913)
  Pallas kernels: 79.6 us -> 72.5 us
    pallas_call x1, Pallas kernels: 79.6 us -> 72.5 us  [per_device(): pl.pallas_call(functools.partial(kernel, n_tm, n_sp), out_shape=(jax.Shap...]
where the time goes in v3:
time: 75.4 us; the launch traced here: 75.3 us
  Pallas kernels  72.5 us (96%)
  local copies, waits for them, and re-layouts  2.16 us (3%)
    pallas_call x1, Pallas kernels, per_device(): pl.pallas_call(functools.partial(kernel, n_tm, n_sp), out_shape=(jax.Shap...  72.5 us
    unnamed x4, local copies, waits for them, and re-layouts  2.16 us

profile of v3, /device:TPU:26, one launch (start us, length us, event | category | flops | bytes accessed | tf_op | source)
XLA Modules:
  0.0 75.3 jit_solution(3968629942118742625)
XLA Ops:
  0.6 72.5 %parareal.1 = (f32[1,3,8,1024]{3,2,1,0:T(8,128)}, f32[1,8,1024]{2,1,0:T(8,128)}) custom-call(f32[3,8,1024]{2,1,0:T(8,128)} %u_hbm.1, f32[8,1024]{1,0:T(8,128)} %s_hbm.1, f32[8,1024]{1,0:T(8,128)} %d_hbm.1, f32[3,8,1024]{2,1,0:T(8,128)} %f_hbm.1, f32[3,3,8,1024]{3,2,1,0:T(8,128)} %down_hbm.1, f32[3,3,8,1024]{3,2,1,0:T(8,128)} %lat_hbm.1, f32[64]{0:T(128)} %heat_hbm.1, ...), custom_call_target="tpu_custom_call" | custom-call | tf_op jit(solution)/shard_map/parareal/pallas_call | solution.py:523
  73.1 0.0 copy-start
  73.1 1.5 %copy.12 = f32[1,3,8,1024]{3,2,1,0:T(8,128)} copy(f32[1,3,8,1024]{3,2,1,0:T(8,128)} %get-tuple-element.4) | data formatting | bytes 196608
  74.7 0.0 copy-done
  74.7 0.6 copy.13
Async XLA Ops:
  73.1 1.6 %copy-start = (f32[1,8,1024]{2,1,0:T(8,128)S(1)}, f32[1,8,1024]{2,1,0:T(8,128)}, u32[]{:S(2)}) copy-start(f32[1,8,1024]{2,1,0:T(8,128)} %get-tuple-element.5) | copy-start | bytes 98308

commit v4 on v3

--- a/solution.py
+++ b/solution.py
@@ -236,7 +236,7 @@
         def store_s(r, c, x):
             U[3, span(r, c), :] = x
 
-        creep(load, store_s, t, h, 1, ROWS - 2, 8)
+        creep(load, store_s, t, h, 1, ROWS - 2, 12)
         th = h * t
 
         def first(r, v, cv):
@@ -279,11 +279,11 @@
             U[k, span(ABOVE, 8), :] = XH[slot, 0, k]
             U[k, span(BELOW, 8), :] = XH[slot, 1, k]
 
-    def coarse_own():
+    def coarse_own(src):
         t = mean_heat(n)
 
         def load(k, r, c):
-            return U[k, span(r, c), :]
+            return src[k, span(r, c), :]
 
         def store_s(r, c, x):
             GU[3, span(r - OWN, c), :] = x
@@ -295,7 +295,7 @@
             for a in range(3):
                 GU[a, at(r - OWN), :] = MASS * v[a] + g[a]
 
-        stencil(lambda b, r: U[b, at(r), :], OWN, OWN + 8, emit)
+        stencil(lambda b, r: src[b, at(r), :], OWN, OWN + 8, emit)
 
     def coarse_step(m, _):
         t = mean_heat(m)
@@ -306,7 +306,7 @@
         def store_s(r, c, x):
             U[3, span(r, c), :] = x
 
-        creep(load, store_s, t, 2.0 * TICK, 1, ROWS - 2, 8)
+        creep(load, store_s, t, 2.0 * TICK, 1, ROWS - 2, 12)
 
         def emit(r, v, cv):
             g = force(r, v, cv, 2.0 * TICK * t)
@@ -320,11 +320,11 @@
 
     @pl.when(n == 1)
     def _():
-        coarse_own()
+        coarse_own(U)
 
     @pl.when(n > 1)
     def _():
-        exchange(0, 15, 4, coarse_own)
+        exchange(0, 15, 4, lambda: coarse_own(U))
 
     odd = lax.rem(n, 2) == 1
     even = (lax.rem(n, 2) == 0) & (n > 0)
@@ -383,7 +383,12 @@
             def tick(i, _):
                 @pl.when(i == 1)
                 def _():
-                    exchange(1 + 2 * p, 17 + 4 * p, 3)
+                    def meanwhile():
+                        @pl.when(even & (p == 1))
+                        def _():
+                            coarse_own(VIN.at[0])
+
+                    exchange(1 + 2 * p, 17 + 4 * p, 3, meanwhile)
 
                 fine_tick(heat_of(n, i))
                 return 0
@@ -445,9 +450,9 @@
                 VOUT[p, k] = U[k, span(OWN, 8), :]
 
         def pass_on():
-            @pl.when(n > 0)
+            @pl.when((n > 0) & jnp.logical_not(even & (p == 0)))
             def _():
-                coarse_own()
+                coarse_own(U)
                 for a in range(3):
                     VOUT[p, a] = GU[a] + C[p, a]
                 VOUT[p, 3] = GU[3] * C[p, 3]
@@ -457,16 +462,27 @@
                 for c in to_first():
                     c.start()
 
+            next_first = (n == n_tm - 3) & (p == 0)
+
+            @pl.when(next_first)
+            def _():
+                for c in to_next(0):
+                    c.start()
+
             @pl.when(hands_on)
             def _():
                 for c in to_second(p):
                     c.start()
 
-            for q in range(2):
-                @pl.when(hands_on & (p == q))
-                def _():
-                    for c in to_next(q):
-                        c.start()
+            @pl.when(hands_on & (n < n_tm - 3) & (p == 0))
+            def _():
+                for c in to_next(0):
+                    c.start()
+
+            @pl.when(hands_on & (p == 1))
+            def _():
+                for c in to_next(1):
+                    c.start()
 
         halo_now = joins & (p == 0)
 

time: 75.4 us -> 74.8 us (level)
  no operation moved by 1% of the time
where the time goes in v4:
time: 74.8 us; the launch traced here: 74.7 us
  Pallas kernels  71.9 us (96%)
  local copies, waits for them, and re-layouts  2.16 us (3%)
    pallas_call x1, Pallas kernels, per_device(): pl.pallas_call(functools.partial(kernel, n_tm, n_sp), out_shape=(jax.Shap...  71.9 us
    unnamed x4, local copies, waits for them, and re-layouts  2.16 us

profile of v4, /device:TPU:26, one launch (start us, length us, event | category | flops | bytes accessed | tf_op | source)
XLA Modules:
  0.0 74.7 jit_solution(4134896524027550371)
XLA Ops:
  0.6 71.9 %parareal.1 = (f32[1,3,8,1024]{3,2,1,0:T(8,128)}, f32[1,8,1024]{2,1,0:T(8,128)}) custom-call(f32[3,8,1024]{2,1,0:T(8,128)} %u_hbm.1, f32[8,1024]{1,0:T(8,128)} %s_hbm.1, f32[8,1024]{1,0:T(8,128)} %d_hbm.1, f32[3,8,1024]{2,1,0:T(8,128)} %f_hbm.1, f32[3,3,8,1024]{3,2,1,0:T(8,128)} %down_hbm.1, f32[3,3,8,1024]{3,2,1,0:T(8,128)} %lat_hbm.1, f32[64]{0:T(128)} %heat_hbm.1, ...), custom_call_target="tpu_custom_call" | custom-call | tf_op jit(solution)/shard_map/parareal/pallas_call | solution.py:539
  72.5 0.0 copy-start
  72.5 1.5 %copy.12 = f32[1,3,8,1024]{3,2,1,0:T(8,128)} copy(f32[1,3,8,1024]{3,2,1,0:T(8,128)} %get-tuple-element.4) | data formatting | bytes 196608
  74.1 0.0 copy-done
  74.1 0.6 copy.13
Async XLA Ops:
  72.5 1.6 %copy-start = (f32[1,8,1024]{2,1,0:T(8,128)S(1)}, f32[1,8,1024]{2,1,0:T(8,128)}, u32[]{:S(2)}) copy-start(f32[1,8,1024]{2,1,0:T(8,128)} %get-tuple-element.5) | copy-start | bytes 98308

commit v5 on v4

--- a/solution.py
+++ b/solution.py
@@ -66,9 +66,6 @@
              (u_hbm, u_in), (s_hbm, s_in), (d_hbm, d_in), (f_hbm, f_in)]
         )
     ]
-    for c in loads:
-        c.start()
-
     barrier = pltpu.get_barrier_semaphore()
     peers = [(lax.rem(n + d, n_tm), sp) for d in range(1, n_tm)]
     for d in (0, 1, 2, n_tm - 2, n_tm - 1):
@@ -77,6 +74,9 @@
     peers += [(n, up2), (n, dn2)]
     for peer in peers:
         pl.semaphore_signal(barrier, inc=1, device_id=peer, device_id_type=MESH)
+
+    for c in loads:
+        c.start()
 
     def copy(src, dst, sem, who):
         return pltpu.make_async_remote_copy(

time: 74.8 us -> 74.8 us (level)
  no operation moved by 1% of the time
where the time goes in v5:
time: 74.8 us; the launch traced here: 74.7 us
  Pallas kernels  71.9 us (96%)
  local copies, waits for them, and re-layouts  2.16 us (3%)
    pallas_call x1, Pallas kernels, per_device(): pl.pallas_call(functools.partial(kernel, n_tm, n_sp), out_shape=(jax.Shap...  71.9 us
    unnamed x4, local copies, waits for them, and re-layouts  2.16 us

profile of v5, /device:TPU:26, one launch (start us, length us, event | category | flops | bytes accessed | tf_op | source)
XLA Modules:
  0.0 74.7 jit_solution(3008194200389379408)
XLA Ops:
  0.6 71.9 %parareal.1 = (f32[1,3,8,1024]{3,2,1,0:T(8,128)}, f32[1,8,1024]{2,1,0:T(8,128)}) custom-call(f32[3,8,1024]{2,1,0:T(8,128)} %u_hbm.1, f32[8,1024]{1,0:T(8,128)} %s_hbm.1, f32[8,1024]{1,0:T(8,128)} %d_hbm.1, f32[3,8,1024]{2,1,0:T(8,128)} %f_hbm.1, f32[3,3,8,1024]{3,2,1,0:T(8,128)} %down_hbm.1, f32[3,3,8,1024]{3,2,1,0:T(8,128)} %lat_hbm.1, f32[64]{0:T(128)} %heat_hbm.1, ...), custom_call_target="tpu_custom_call" | custom-call | tf_op jit(solution)/shard_map/parareal/pallas_call | solution.py:539
  72.5 0.0 copy-start
  72.5 1.5 %copy.12 = f32[1,3,8,1024]{3,2,1,0:T(8,128)} copy(f32[1,3,8,1024]{3,2,1,0:T(8,128)} %get-tuple-element.4) | data formatting | bytes 196608
  74.1 0.0 copy-done
  74.1 0.6 copy.13
Async XLA Ops:
  72.5 1.6 %copy-start = (f32[1,8,1024]{2,1,0:T(8,128)S(1)}, f32[1,8,1024]{2,1,0:T(8,128)}, u32[]{:S(2)}) copy-start(f32[1,8,1024]{2,1,0:T(8,128)} %get-tuple-element.5) | copy-start | bytes 98308
